TPU v7x, 32 devices: a whole 2x2x4 slice. The times are simulated.
32 devices in a mesh: seq: 8 (over z, y), item: 4 (over x, core).
Axes of the slice: x: 2, y: 2, z: 4, core: 2. Of those that a mesh axis runs over, the one named last changes fastest.
Arguments:
- inputs: float32 [1024, 24, 768], P('seq', 'item'), may hold values from -6 to 6
- w_in: float32 [768, 3072], replicated, may hold values from -0.21875 to 0.21875
- c_in: float32 [3072], replicated, may hold values from -3 to 3
- w_out: float32 [3072, 768], replicated, may hold values from -0.109375 to 0.109375
- c_out: float32 [768], replicated, may hold values from -3 to 3
- gain_mix: float32 [768], replicated, may hold values from 0.5 to 1.5
- bias_mix: float32 [768], replicated, may hold values from -3 to 3
- gain_out: float32 [768], replicated, may hold values from 0.5 to 1.5
- bias_out: float32 [768], replicated, may hold values from -3 to 3
- cotangent: float32 [1024, 24, 768], P('seq', 'item'), may hold values from -6 to 6
Outputs:
- output: float32 [1024, 24, 768], P('seq', 'item')
- grad_inputs: float32 [1024, 24, 768], P('seq', 'item')
- grad_w_in: float32 [768, 3072], P('seq')
- grad_c_in: float32 [3072], P('seq')
- grad_w_out: float32 [3072, 768], P('seq')
- grad_c_out: float32 [768], P('seq')
- grad_gain_mix: float32 [768], P('seq')
- grad_bias_mix: float32 [768], P('seq')
- grad_gain_out: float32 [768], P('seq')
- grad_bias_out: float32 [768], P('seq')
All inputs are finite; a program needn't handle non-finite values.
Results may differ from a plain program's by a relative error of at most 0.015.
Values may be sent and summed in bfloat16 or wider, within the bound.
A program may use at most 256 MiB of HBM per device.

v0:
```python
import math

import jax
import jax.numpy as jnp
from jax import lax
from jax.sharding import PartitionSpec as P


def table_block(row_ids, col_ids, period):
    products = row_ids[:, None] * col_ids[None, :] % period
    angles = products.astype(jnp.float32) * (2.0 * math.pi / period)
    return (jnp.cos(angles).astype(jnp.bfloat16), jnp.sin(angles).astype(jnp.bfloat16))


def plain_dot(left, right):
    return jnp.dot(left, right, preferred_element_type=jnp.float32)


def rows_dot(left, right):
    return lax.dot_general(
        left, right, (((0,), (0,)), ((), ())), preferred_element_type=jnp.float32
    )


def cols_dot(left, right):
    return lax.dot_general(
        left, right, (((1,), (1,)), ((), ())), preferred_element_type=jnp.float32
    )


def layer_norm(values, scales, shifts):
    average = jnp.mean(values, axis=-1, keepdims=True)
    centered = values - average
    variance = jnp.mean(centered * centered, axis=-1, keepdims=True)
    return centered * lax.rsqrt(variance + 1e-05) * scales + shifts


def gelu_exact(values):
    return jax.nn.gelu(values, approximate=False)


def body(inputs, w_in, c_in, w_out, c_out, gain_mix, bias_mix, gain_out, bias_out, cotangent):
    local_len, per_dev, features = inputs.shape
    merged = per_dev * features
    period = local_len * lax.axis_size("seq")
    unit_scale = 1.0 / math.sqrt(period * features)
    own_rows = lax.axis_index("seq") * local_len + jnp.arange(local_len, dtype=jnp.int32)
    feat_ids = jnp.arange(features, dtype=jnp.int32)
    cos_hid, sin_hid = table_block(feat_ids, feat_ids, features)
    tokens = inputs.reshape(-1, features)
    tokens_low = tokens.astype(jnp.bfloat16)
    cos_part = (
        plain_dot(tokens_low, cos_hid).astype(jnp.bfloat16).reshape(local_len, per_dev, features)
    )
    sin_part = (
        plain_dot(tokens_low, sin_hid).astype(jnp.bfloat16).reshape(local_len, per_dev, features)
    )
    pieces = (
        lax.all_gather(cos_part, "seq", axis=0, tiled=True),
        lax.all_gather(sin_part, "seq", axis=0, tiled=True),
    )
    col_ids = jnp.arange(pieces[0].shape[0], dtype=jnp.int32)
    cos_blk, sin_blk = table_block(own_rows, col_ids, period)
    mixed = plain_dot(cos_blk, pieces[0].reshape(pieces[0].shape[0], -1)) - plain_dot(
        sin_blk, pieces[1].reshape(pieces[1].shape[0], -1)
    )
    mixed = (mixed * unit_scale).reshape(-1, features)
    hidden, pull_mix = jax.vjp(layer_norm, tokens + mixed, gain_mix, bias_mix)
    hidden_low = hidden.astype(jnp.bfloat16)
    w_in_low = w_in.astype(jnp.bfloat16)
    w_out_low = w_out.astype(jnp.bfloat16)
    pre = plain_dot(hidden_low, w_in_low) + c_in
    act, pull_gelu = jax.vjp(gelu_exact, pre)
    act_low = act.astype(jnp.bfloat16)
    branch = plain_dot(act_low, w_out_low) + c_out
    output, pull_out = jax.vjp(layer_norm, hidden + branch, gain_out, bias_out)
    g_sum2, grad_gain_out, grad_bias_out = pull_out(cotangent.reshape(-1, features))
    g_branch = g_sum2.astype(jnp.bfloat16)
    grad_c_out = jnp.sum(g_branch.astype(jnp.float32), axis=0)
    grad_w_out = rows_dot(act_low, g_branch)
    (g_act,) = pull_gelu(cols_dot(g_branch, w_out_low))
    g_pre = g_act.astype(jnp.bfloat16)
    grad_c_in = jnp.sum(g_pre.astype(jnp.float32), axis=0)
    grad_w_in = rows_dot(hidden_low, g_pre)
    g_hidden = g_sum2 + cols_dot(g_pre, w_in_low)
    g_sum1, grad_gain_mix, grad_bias_mix = pull_mix(g_hidden)
    g_mixed = g_sum1.astype(jnp.bfloat16).reshape(local_len, per_dev, features)
    empty = jnp.zeros((local_len, merged), jnp.float32)
    piece = lax.all_gather(g_mixed, "seq", axis=0, tiled=True)
    row_ids = jnp.arange(piece.shape[0], dtype=jnp.int32)
    cos_blk, sin_blk = table_block(row_ids, own_rows, period)
    flat = piece.reshape(piece.shape[0], -1)
    cycle_gc = rows_dot(cos_blk, flat)
    cycle_gs = (empty, empty)[1] - rows_dot(sin_blk, flat)
    g_cos = (cycle_gc * unit_scale).astype(jnp.bfloat16).reshape(-1, features)
    g_sin = (cycle_gs * unit_scale).astype(jnp.bfloat16).reshape(-1, features)
    grad_inputs = g_sum1 + cols_dot(g_cos, cos_hid) + cols_dot(g_sin, sin_hid)
    shards = (
        lax.psum_scatter(
            grad_w_in.astype(jnp.bfloat16), "seq", scatter_dimension=0, tiled=True
        ).astype(jnp.float32),
        lax.psum_scatter(
            grad_c_in.astype(jnp.bfloat16), "seq", scatter_dimension=0, tiled=True
        ).astype(jnp.float32),
        lax.psum_scatter(
            grad_w_out.astype(jnp.bfloat16), "seq", scatter_dimension=0, tiled=True
        ).astype(jnp.float32),
        lax.psum_scatter(
            grad_c_out.astype(jnp.bfloat16), "seq", scatter_dimension=0, tiled=True
        ).astype(jnp.float32),
        lax.psum_scatter(
            grad_gain_mix.astype(jnp.bfloat16), "seq", scatter_dimension=0, tiled=True
        ).astype(jnp.float32),
        lax.psum_scatter(
            grad_bias_mix.astype(jnp.bfloat16), "seq", scatter_dimension=0, tiled=True
        ).astype(jnp.float32),
        lax.psum_scatter(
            grad_gain_out.astype(jnp.bfloat16), "seq", scatter_dimension=0, tiled=True
        ).astype(jnp.float32),
        lax.psum_scatter(
            grad_bias_out.astype(jnp.bfloat16), "seq", scatter_dimension=0, tiled=True
        ).astype(jnp.float32),
    )
    summed = (
        lax.psum(shards[0].astype(jnp.bfloat16), "item").astype(jnp.float32),
        lax.psum(shards[1].astype(jnp.bfloat16), "item").astype(jnp.float32),
        lax.psum(shards[2].astype(jnp.bfloat16), "item").astype(jnp.float32),
        lax.psum(shards[3].astype(jnp.bfloat16), "item").astype(jnp.float32),
        lax.psum(shards[4].astype(jnp.bfloat16), "item").astype(jnp.float32),
        lax.psum(shards[5].astype(jnp.bfloat16), "item").astype(jnp.float32),
        lax.psum(shards[6].astype(jnp.bfloat16), "item").astype(jnp.float32),
        lax.psum(shards[7].astype(jnp.bfloat16), "item").astype(jnp.float32),
    )
    return (
        output.reshape(inputs.shape),
        grad_inputs.reshape(inputs.shape),
        summed[0],
        summed[1],
        summed[2],
        summed[3],
        summed[4],
        summed[5],
        summed[6],
        summed[7],
    )


def solution(mesh):
    placed = (
        P("seq", "item", None),
        P(),
        P(),
        P(),
        P(),
        P(),
        P(),
        P(),
        P(),
        P("seq", "item", None),
    )
    return jax.shard_map(
        body,
        mesh=mesh,
        in_specs=placed,
        out_specs=(
            P("seq", "item", None),
            P("seq", "item", None),
            P("seq", None),
            P("seq"),
            P("seq", None),
            P("seq"),
            P("seq"),
            P("seq"),
            P("seq"),
            P("seq"),
        ),
        check_vma=False,
    )
```

profile of v0, /device:TPU:0, one launch (start us, length us, event | category | flops | bytes accessed | tf_op | source)
XLA Modules:
  0.0 825.0 jit_solution(8296600456836356922)
XLA Ops:
  7.2 3.1 copy.35
  10.3 1.6 reshape.156
  11.9 11.7 %fusion.30 = bf16[768,768]{1,0:T(8,128)(2,1)S(1)} fusion(f32[768,768]{1,0:T(8,128)} %reshape.156), kind=kOutput, calls=%fused_computation.62 | convolution fusion | flops 913047552 | bytes 3538944 | tf_op jit(solution)/shard_map/dot_general | solution.py:16
  23.6 1.4 reshape.157
  25.0 2.8 copy.36
  27.9 10.1 %fusion.31 = bf16[768,768]{1,0:T(8,128)(2,1)S(1)} fusion(f32[768,768]{1,0:T(8,128)S(1)} %copy-done.4), kind=kOutput, calls=%fused_computation.63 | convolution fusion | flops 913047552 | bytes 3538944 | tf_op jit(solution)/shard_map/dot_general | solution.py:16
  38.0 1.4 reshape.159
  39.3 2.8 copy.38
  42.5 2.0 copy.41
  44.5 3.1 copy.44
  47.5 1.6 reshape.164
  49.1 119.5 %all-gather.4.cloned.1.call-done = bf16[1024,6,768]{2,0,1:T(8,128)(2,1)} async-done(((bf16[128,6,768]{2,0,1:T(8,128)(2,1)}), bf16[1024,6,768]{2,0,1:T(8,128)(2,1)}) %all-gather.4.cloned.1.call-update) | async-done | bytes 9437200 | tf_op jit(solution)/shard_map/all_gather | solution.py:59
  168.6 12.8 %copy.37 = bf16[1024,6,768]{0,2,1:T(8,128)(2,1)} copy(bf16[1024,6,768]{2,0,1:T(8,128)(2,1)} %all-gather.4.cloned.1.call-done) | data formatting | bytes 18874368 | tf_op jit(solution)/shard_map/all_gather | solution.py:59
  181.5 10.1 %fusion.47 = f32[128,4608]{1,0:T(8,128)} fusion(bf16[1024,4608]{0,1:T(8,128)(2,1)} %bitcast.22, s32[128]{0:T(128)S(1)} %iota_add_fusion), kind=kOutput, calls=%fused_computation.89 | convolution fusion | flops 1209925632 | bytes 11796992 | tf_op jit(solution)/shard_map/dot_general | solution.py:16
  191.6 116.1 %all-gather.6.cloned.1.call-done = bf16[1024,6,768]{2,0,1:T(8,128)(2,1)} async-done(((bf16[128,6,768]{2,0,1:T(8,128)(2,1)}), bf16[1024,6,768]{2,0,1:T(8,128)(2,1)}) %all-gather.6.cloned.1.call-update) | async-done | bytes 9437200 | tf_op jit(solution)/shard_map/all_gather | solution.py:60
  307.7 12.7 %copy.39 = bf16[1024,6,768]{0,2,1:T(8,128)(2,1)} copy(bf16[1024,6,768]{2,0,1:T(8,128)(2,1)} %all-gather.6.cloned.1.call-done) | data formatting | bytes 18874368 | tf_op jit(solution)/shard_map/all_gather | solution.py:60
  320.3 9.4 %fusion.7 = f32[128,4608]{1,0:T(8,128)S(1)} fusion(f32[128,4608]{1,0:T(8,128)} %fusion.47, bf16[1024,4608]{0,1:T(8,128)(2,1)} %bitcast.21, s32[128]{0:T(128)S(1)} %iota_add_fusion), kind=kOutput, calls=%fused_computation.21 | convolution fusion | flops 1211105280 | bytes 14156288 | tf_op jit(solution)/shard_map/dot_general | solution.py:16
  329.7 2.0 copy.40
  331.7 2.0 reshape.161
  333.7 2.6 fusion.87
  337.2 2.8 add_subtract_fusion
  340.1 28.1 %multiply_convert_fusion = (bf16[768,3072]{1,0:T(8,128)(2,1)S(1)}, f32[768,3072]{1,0:T(8,128)}, f32[768,3072]{1,0:T(8,128)}) fusion(f32[3072]{0:T(1024)S(1)} %copy-done.17, f32[768,3072]{1,0:T(8,128)} %param.11, f32[768,768]{1,0:T(8,128)S(1)} %add_subtract_fusion, f32[768]{0:T(1024)S(1)} %copy-done.19, f32[768]{0:T(1024)S(1)} %copy-done.11, f32[768]{0:T(1024)S(1)} %rsqrt.20), kind=kOutput, calls=%fused_computation.3 | convolution fusion | flops 3784310784 | bytes 35410944 | tf_op jit(solution)/shard_map/dot_general | solution.py:16
  368.2 4.1 fusion.88
  372.3 0.4 multiply_reduce_fusion.4
  372.8 1.2 copy-done
  374.0 0.9 multiply_reduce_fusion
  374.9 2.4 fusion.85
  377.3 1.4 copy-done.7
  378.7 0.9 fusion.83
  379.6 5.8 convolution_convert_fusion
  385.5 14.4 %fusion.89 = (bf16[3072]{0:T(1024)(128)(2,1)}, bf16[768,3072]{1,0:T(8,128)(2,1)S(1)}) fusion(f32[768,3072]{1,0:T(8,128)} %get-tuple-element.66, bf16[768,768]{1,0:T(8,128)(2,1)S(1)} %get-tuple-element.60, f32[3072,768]{1,0:T(8,128)} %param.13, f32[768,3072]{1,0:T(8,128)} %get-tuple-element.70, f32[3072]{0:T(1024)} %param.12), kind=kOutput, calls=%fused_computation.133 | convolution fusion | flops 3663983616 | bytes 34228224 | tf_op jit(solution)/shard_map/dot_general | solution.py:26
  399.9 2.1 copy-done.22
  402.0 5.9 convolution_convert_fusion.1
  407.9 0.6 copy-done.13
  408.6 11.8 %multiply_reduce_fusion.1 = (bf16[768]{0:T(1024)(128)(2,1)S(1)}, f32[768]{0:T(1024)S(1)}, bf16[768]{0:T(1024)(128)(2,1)S(1)}, f32[768,768]{1,0:T(8,128)}) fusion(f32[768,768]{1,0:T(8,128)S(1)} %add_subtract_fusion, f32[768]{0:T(1024)S(1)} %rsqrt.20, f32[768]{0:T(1024)S(1)} %copy-done.13, bf16[768,3072]{1,0:T(8,128)(2,1)} %copy-done.22, ...), kind=kOutput, calls=%fused_computation.32 | convolution fusion | flops 3631544064 | bytes 21249024 | tf_op jit(solution)/shard_map/dot_general | solution.py:26
  420.3 58.8 %reduce-scatter.5.cloned.1.call-done = bf16[384,768]{1,0:T(8,128)(2,1)} async-done(((bf16[3072,768]{1,0:T(8,128)(2,1)}), bf16[384,768]{1,0:T(8,128)(2,1)}) %reduce-scatter.5.cloned.1.call-update) | async-done | bytes 589840 | tf_op jit(solution)/shard_map/reduce_scatter | solution.py:105
  479.2 98.5 %reduce-scatter.3.cloned.1.call-done = bf16[96,3072]{1,0:T(8,128)(2,1)} async-done(((bf16[768,3072]{1,0:T(8,128)(2,1)}), bf16[96,3072]{1,0:T(8,128)(2,1)}) %reduce-scatter.3.cloned.1.call-update) | async-done | bytes 589840 | tf_op jit(solution)/shard_map/reduce_scatter | solution.py:99
  577.8 2.4 fusion.84
  580.2 1.4 copy-done.1
  581.8 1.6 reshape.165
  583.4 2.8 copy.45
  586.8 0.6 dynamic-slice
  588.7 35.9 %all-reduce.6 = (bf16[3072]{0:T(1024)(128)(2,1)S(1)}, bf16[768]{0:T(1024)(128)(2,1)S(1)}, bf16[768]{0:T(1024)(128)(2,1)S(1)}, bf16[768]{0:T(1024)(128)(2,1)S(1)}...) all-reduce(bf16[3072]{0:T(1024)(128)(2,1)S(1)} %copy-done.10, ...), channel_id=3, replica_groups=mesh['seq'=8,'item'=4] {'seq'}, use_global_device_ids=true, to_apply=%region_11.12.clone | all-reduce | flops 6912 | bytes 27648
  625.1 5.6 all-reduce.7
  630.8 0.6 convert_element_type.166
  631.3 0.5 convert_element_type.169
  631.9 0.5 convert_element_type.171
  632.4 0.5 convert_element_type.173
  632.9 0.5 convert_element_type.175
  633.4 0.5 convert_element_type.177
  633.9 2.5 reshape.163
  636.4 2.1 copy.47
  638.5 2.2 convert_element_type.165
  640.7 2.2 convert_element_type.168
  642.8 114.7 %all-gather.8.cloned.1.call-done = bf16[1024,6,768]{2,0,1:T(8,128)(2,1)} async-done(((bf16[128,6,768]{2,0,1:T(8,128)(2,1)}), bf16[1024,6,768]{2,0,1:T(8,128)(2,1)}) %all-gather.8.cloned.1.call-update) | async-done | bytes 9437200 | tf_op jit(solution)/shard_map/all_gather | solution.py:89
  757.6 12.4 %copy.46 = bf16[1024,6,768]{0,2,1:T(8,128)(2,1)} copy(bf16[1024,6,768]{2,0,1:T(8,128)(2,1)} %all-gather.8.cloned.1.call-done) | data formatting | bytes 18874368 | tf_op jit(solution)/shard_map/all_gather | solution.py:89
  769.9 8.8 %fusion.9 = bf16[128,4608]{1,0:T(8,128)(2,1)S(1)} fusion(bf16[1024,4608]{0,1:T(8,128)(2,1)} %bitcast.24, s32[128]{0:T(128)S(1)} %copy-done.16), kind=kOutput, calls=%fused_computation.23 | convolution fusion | flops 1211105280 | bytes 10617344 | tf_op jit(solution)/shard_map/dot_general | solution.py:20
  778.7 5.0 fusion.8
  783.7 2.0 reshape.167
  785.7 12.6 %fusion.32 = f32[768,768]{1,0:T(8,128)} fusion(bf16[768,768]{1,0:T(8,128)(2,1)} %reshape.167), kind=kOutput, calls=%fused_computation.64 | convolution fusion | flops 911867904 | bytes 3538944 | tf_op jit(solution)/shard_map/dot_general | solution.py:26
  798.3 2.0 reshape.168
  800.3 12.8 %add_add_fusion.2 = f32[768,768]{1,0:T(8,128)} fusion(f32[768,768]{1,0:T(8,128)} %fusion.32, f32[768,768]{1,0:T(8,128)S(1)} %copy-done.2, bf16[768,768]{1,0:T(8,128)(2,1)} %reshape.168, f32[768]{0:T(1024)S(1)} %negate_multiply_fusion.1), kind=kOutput, calls=%fused_computation.33 | convolution fusion | flops 913637376 | bytes 8260608 | tf_op jit(solution)/shard_map/dot_general | solution.py:26
  813.1 2.5 reshape.169
  815.5 2.1 copy.48
  (84 shorter events, 2.7 us)
Async XLA Ops:
  7.2 161.5 %all-gather.4.cloned.1.call-start = ((), (), s32[]{:S(2)}) async-start(), calls=%async_computation.2 | async-start | bytes 10616832 | tf_op jit(solution)/shard_map/all_gather | solution.py:59
  25.0 2.9 copy-start.4
  27.8 279.9 %all-gather.6.cloned.1.call-start = ((), (), s32[]{:S(2)}) async-start(), calls=%async_computation.3 | async-start | bytes 10616832 | tf_op jit(solution)/shard_map/all_gather | solution.py:60
  39.3 3.1 copy-start.5
  42.2 437.0 %reduce-scatter.5.cloned.1.call-start = ((), (), s32[]{:S(2)}) async-start(), calls=%async_computation.6 | async-start | bytes 5308416 | tf_op jit(solution)/shard_map/reduce_scatter | solution.py:105
  49.1 271.2 %copy-start.15 = (s32[128]{0:T(128)}, s32[128]{0:T(128)S(1)}, u32[]{:S(2)}) copy-start(s32[128]{0:T(128)S(1)} %iota_add_fusion) | copy-start | bytes 1540
  337.1 2.9 copy-start.11
  337.1 2.9 copy-start.17
  337.2 2.9 copy-start.19
  337.2 31.0 %slice-start = ((s8[9437184]{0:T(1024)(128)(4,1)}), s8[4194304]{0:T(1024)(128)(4,1)S(1)}, s32[]{:S(2)}) async-start(s8[9437184]{0:T(1024)(128)(4,1)} %bitcast.26), calls=%async_computation.8 | async-start | bytes 8388608
  340.0 28.2 %slice-start.1 = ((s8[9437184]{0:T(1024)(128)(4,1)}), s8[4194304]{0:T(1024)(128)(4,1)S(1)}, s32[]{:S(2)}) async-start(s8[9437184]{0:T(1024)(128)(4,1)} %bitcast.26), calls=%async_computation.9 | async-start | bytes 8388608
  340.0 28.2 %slice-start.2 = ((s8[9437184]{0:T(1024)(128)(4,1)}), s8[1048576]{0:T(1024)(128)(4,1)S(1)}, s32[]{:S(2)}) async-start(s8[9437184]{0:T(1024)(128)(4,1)} %bitcast.26), calls=%async_computation.10 | async-start | bytes 2097152
  340.0 28.1 %copy-start.18 = (f32[768]{0:T(1024)S(1)}, f32[768]{0:T(1024)}, u32[]{:S(2)}) copy-start(f32[768]{0:T(1024)} %param.14) | copy-start | bytes 9220
  372.3 1.7 copy-start
  372.3 1.7 copy-start.8
  374.0 0.9 copy-start.14
  377.3 1.4 copy-start.7
  385.4 192.3 %reduce-scatter.3.cloned.1.call-start = ((), (), s32[]{:S(2)}) async-start(), calls=%async_computation.5 | async-start | bytes 5308416 | tf_op jit(solution)/shard_map/reduce_scatter | solution.py:99
  385.5 16.5 %copy-start.12 = (f32[768]{0:T(1024)S(1)}, f32[768]{0:T(1024)}, u32[]{:S(2)}) copy-start(f32[768]{0:T(1024)} %param.15) | copy-start | bytes 9220
  385.5 16.5 %copy-start.20 = (f32[768]{0:T(1024)S(1)}, f32[768]{0:T(1024)}, u32[]{:S(2)}) copy-start(f32[768]{0:T(1024)} %param.16) | copy-start | bytes 9220
  399.8 2.1 copy-start.22
  407.9 0.7 copy-start.13
  407.9 230.6 %all-reduce.11.cloned.1.call-start = ((), (), s32[]{:S(2)}) async-start(), calls=%async_computation.7 | async-start | bytes 2359296 | tf_op jit(solution)/shard_map/psum | solution.py:125
  577.7 179.8 %all-gather.8.cloned.1.call-start = ((), (), s32[]{:S(2)}) async-start(), calls=%async_computation.4 | async-start | bytes 10616832 | tf_op jit(solution)/shard_map/all_gather | solution.py:89
  580.2 1.4 copy-start.1
  583.4 2.8 copy-start.6
  586.2 0.7 copy-start.21
  586.2 2.5 copy-start.9
  586.2 2.5 copy-start.10
  642.8 127.1 %copy-start.16 = (s32[128]{0:T(128)S(1)}, s32[128]{0:T(128)}, u32[]{:S(2)}) copy-start(s32[128]{0:T(128)} %copy-done.15) | copy-start | bytes 1540
  769.9 8.8 %copy-start.3 = (bf16[1024,6,768]{0,2,1:T(8,128)(2,1)S(1)}, bf16[1024,6,768]{0,2,1:T(8,128)(2,1)}, u32[]{:S(2)}) copy-start(bf16[1024,6,768]{0,2,1:T(8,128)(2,1)} %copy.46) | copy-start | bytes 28311556
  785.7 14.6 %copy-start.2 = (f32[768,768]{1,0:T(8,128)S(1)}, f32[768,768]{1,0:T(8,128)}, u32[]{:S(2)}) copy-start(f32[768,768]{1,0:T(8,128)} %copy-done.1) | copy-start | bytes 7077892
Sparse Core Ops, SparseCore 0:
  27.9 140.6 all-gather.3
  171.4 136.2 all-gather.5
  385.5 93.5 reduce-scatter.4
  482.7 94.9 reduce-scatter.2
  580.0 37.2 all-reduce.10
  619.3 138.2 all-gather.7
where the time goes:
time: 833 us; the launch traced here: 825 us
  waiting for transfers between devices  508 us (61%)
  matrix products  151 us (18%)
  local copies, waits for them, and re-layouts  87.7 us (11%)
  blocking collectives  41.6 us (5%)
  other arithmetic  20.5 us (2%)
  between operations  16.3 us (2%)
    all_gather x1, waiting for transfers between devices, body(): lax.all_gather(cos_part, 'seq', axis=0, tiled=True)  119 us
    all_gather x1, waiting for transfers between devices, body(): lax.all_gather(sin_part, 'seq', axis=0, tiled=True)  116 us
    all_gather x1, waiting for transfers between devices, body(): piece = lax.all_gather(g_mixed, 'seq', axis=0, tiled=True)  115 us
    reduce_scatter x1, waiting for transfers between devices, body(): lax.psum_scatter(grad_w_in.astype(jnp.bfloat16), 'seq', scatter_dimension...  98.5 us
    dot_general x6, matrix products, plain_dot(): return jnp.dot(left, right, preferred_element_type=jnp.float32)  73.5 us
    reduce_scatter x1, waiting for transfers between devices, body(): lax.psum_scatter(grad_w_out.astype(jnp.bfloat16), 'seq', scatter_dimensio...  58.8 us
    dot_general x4, matrix products, cols_dot(): lax.dot_general(left, right, (((1,), (1,)), ((), ())), preferred_element_...  51.6 us
    unnamed x1, blocking collectives  35.9 us
  transfers between devices with their start and end apart: 6, of which 5 were waited for; matrix products, arithmetic and copies ran while one was open for 12% of the time, Pallas kernels for 0%

commit v1 on v0

--- a/solution.py
+++ b/solution.py
@@ -2,6 +2,7 @@
 
 import jax
 import jax.numpy as jnp
+import numpy as np
 from jax import lax
 from jax.sharding import PartitionSpec as P
 
@@ -39,7 +40,7 @@
     return jax.nn.gelu(values, approximate=False)
 
 
-def body(inputs, w_in, c_in, w_out, c_out, gain_mix, bias_mix, gain_out, bias_out, cotangent):
+def gather_body(inputs, w_in, c_in, w_out, c_out, gain_mix, bias_mix, gain_out, bias_out, cotangent):
     local_len, per_dev, features = inputs.shape
     merged = per_dev * features
     period = local_len * lax.axis_size("seq")
@@ -145,6 +146,115 @@
     )
 
 
+def packed_tables(features, parts):
+    half = features // 2
+    share = half // parts
+    index = np.arange(features)
+    forward = np.zeros((features, features), np.float32)
+    unpack = np.zeros((features, features), np.float32)
+    for low in range(half):
+        block, place = divmod(low, share)
+        cos_slot = block * 2 * share + place
+        sin_slot = cos_slot + share
+        angles = (index * low % features).astype(np.float32) * np.float32(2.0 * math.pi / features)
+        forward[cos_slot] = np.cos(angles)
+        unpack[cos_slot, low] = 1.0
+        if low:
+            unpack[cos_slot, features - low] = 1.0
+            forward[sin_slot] = np.sin(angles)
+            unpack[sin_slot, low] = -1.0
+            unpack[sin_slot, features - low] = 1.0
+        else:
+            forward[sin_slot] = 1.0 - 2.0 * (index % 2)
+            unpack[sin_slot, half] = 1.0
+    return forward.astype(jnp.bfloat16), unpack.astype(jnp.bfloat16)
+
+
+def seq_tables(period):
+    index = np.arange(period)
+    angles = (index[:, None] * index[None, :] % period).astype(np.float32)
+    angles = angles * np.float32(2.0 * math.pi / period)
+    return np.cos(angles).astype(jnp.bfloat16), np.sin(angles).astype(jnp.bfloat16)
+
+
+def mix(values, forward, unpack, cos_seq, sin_seq):
+    features = values.shape[2]
+    share = features // lax.axis_size("seq") // 2
+    unit_scale = 1.0 / math.sqrt(cos_seq.shape[0] * features)
+    packed = jnp.einsum("gf,spf->gsp", forward, values, preferred_element_type=jnp.float32)
+    packed = packed.astype(jnp.bfloat16)
+    packed = lax.all_to_all(packed, "seq", 0, 2, tiled=True)
+    by_cos = plain_dot(packed[:share], cos_seq)
+    by_sin = plain_dot(packed[share:], sin_seq)
+    middle = plain_dot(packed[share], cos_seq)
+    first = jnp.where(lax.axis_index("seq") == 0, middle, by_sin[0])
+    turned = jnp.concatenate([by_cos, first[None], by_sin[1:]], axis=0) * unit_scale
+    turned = lax.all_to_all(turned.astype(jnp.bfloat16), "seq", 2, 0, tiled=True)
+    return jnp.einsum("gsp,gl->spl", turned, unpack, preferred_element_type=jnp.float32)
+
+
+def exchange_body(inputs, w_in, c_in, w_out, c_out, gain_mix, bias_mix, gain_out, bias_out, cotangent):
+    local_len, per_dev, features = inputs.shape
+    shape = (per_dev, local_len, features)
+    period = local_len * lax.axis_size("seq")
+    forward, unpack = packed_tables(features, lax.axis_size("seq"))
+    cos_seq, sin_seq = seq_tables(period)
+    held = jnp.swapaxes(inputs, 0, 1)
+    mixed = mix(held.astype(jnp.bfloat16), forward, unpack, cos_seq, sin_seq)
+    tokens = held.reshape(-1, features)
+    mixed = mixed.reshape(-1, features)
+    hidden, pull_mix = jax.vjp(layer_norm, tokens + mixed, gain_mix, bias_mix)
+    hidden_low = hidden.astype(jnp.bfloat16)
+    w_in_low = w_in.astype(jnp.bfloat16)
+    w_out_low = w_out.astype(jnp.bfloat16)
+    pre = plain_dot(hidden_low, w_in_low) + c_in
+    act, pull_gelu = jax.vjp(gelu_exact, pre)
+    act_low = act.astype(jnp.bfloat16)
+    branch = plain_dot(act_low, w_out_low) + c_out
+    output, pull_out = jax.vjp(layer_norm, hidden + branch, gain_out, bias_out)
+    cot = jnp.swapaxes(cotangent, 0, 1).reshape(-1, features)
+    g_sum2, grad_gain_out, grad_bias_out = pull_out(cot)
+    g_branch = g_sum2.astype(jnp.bfloat16)
+    grad_c_out = jnp.sum(g_branch.astype(jnp.float32), axis=0)
+    grad_w_out = rows_dot(act_low, g_branch)
+    (g_act,) = pull_gelu(cols_dot(g_branch, w_out_low))
+    g_pre = g_act.astype(jnp.bfloat16)
+    grad_c_in = jnp.sum(g_pre.astype(jnp.float32), axis=0)
+    grad_w_in = rows_dot(hidden_low, g_pre)
+    g_hidden = g_sum2 + cols_dot(g_pre, w_in_low)
+    g_sum1, grad_gain_mix, grad_bias_mix = pull_mix(g_hidden)
+    back = mix(g_sum1.astype(jnp.bfloat16).reshape(shape), forward, unpack, cos_seq, sin_seq)
+    grad_inputs = g_sum1.reshape(shape) + back
+
+    def reduce_matrix(grad):
+        cut = lax.psum_scatter(grad.astype(jnp.bfloat16), "item", scatter_dimension=1, tiled=True)
+        cut = lax.psum_scatter(cut, "seq", scatter_dimension=0, tiled=True)
+        return lax.all_gather(cut, "item", axis=1, tiled=True).astype(jnp.float32)
+
+    parts = lax.axis_size("seq")
+    vectors = (grad_c_in, grad_c_out, grad_gain_mix, grad_bias_mix, grad_gain_out, grad_bias_out)
+    joined = jnp.concatenate([v.reshape(parts, -1) for v in vectors], axis=1)
+    joined = lax.psum(joined, ("seq", "item"))[lax.axis_index("seq")]
+    cuts, at = [], 0
+    for v in vectors:
+        cuts.append(joined[at : at + v.shape[0] // parts])
+        at += v.shape[0] // parts
+    return (
+        jnp.swapaxes(output.reshape(shape), 0, 1),
+        jnp.swapaxes(grad_inputs, 0, 1),
+        reduce_matrix(grad_w_in),
+        cuts[0],
+        reduce_matrix(grad_w_out),
+        *cuts[1:],
+    )
+
+
+def body(inputs, *rest):
+    if inputs.shape[0] * lax.axis_size("seq") > 2048:
+        return gather_body(inputs, *rest)
+    return exchange_body(inputs, *rest)
+
+
 def solution(mesh):
     placed = (
         P("seq", "item", None),

time: 833 us -> 450 us (0.54)
  waiting for transfers between devices: 508 us -> 137 us
  blocking collectives: 41.6 us -> 142 us
  matrix products: 151 us -> 89.5 us
  local copies, waits for them, and re-layouts: 87.7 us -> 34.9 us
  starting transfers between devices: 0.46 us -> 15.5 us
  other arithmetic: 20.5 us -> 9.61 us
    all_gather x3 -> x0, waiting for transfers between devices: 350 us -> none  [the longest x1 119 us: body(): lax.all_gather(cos_part, 'seq', axis=0, tiled=True)]
    reduce_scatter x2 -> x3, waiting for transfers between devices: 157 us -> 63.7 us  [the longest x1 56.7 us: reduce_matrix(): cut = lax.psum_scatter(cut, 'seq', scatter_dimension=0, tiled=True)]
    psum x1, blocking collectives: 5.64 us -> 74.8 us  [exchange_body(): joined = lax.psum(joined, ('seq', 'item'))[lax.axis_index('seq')]]
    all_to_all x0 -> x3, waiting for transfers between devices: none -> 67.5 us  [the longest x2 67.5 us: mix(): packed = lax.all_to_all(packed, 'seq', 0, 2, tiled=True)]
    all_to_all x0 -> x1, blocking collectives: none -> 52.4 us  [mix(): lax.all_to_all(turned.astype(jnp.bfloat16), 'seq', 2, 0, tiled=True)]
    all_gather x3 -> x0, local copies, waits for them, and re-layouts: 37.9 us -> none  [the longest x1 12.8 us: body(): lax.all_gather(cos_part, 'seq', axis=0, tiled=True)]
    unnamed x1 -> x0, blocking collectives: 35.9 us -> none
    dot_general x6 -> x8, matrix products: 73.5 us -> 40 us  [plain_dot(): return jnp.dot(left, right, preferred_element_type=jnp.float32)]
  transfers between devices with their start and end apart: 6 -> 7, of which waited for: 5 -> 6; matrix products, arithmetic and copies ran while one was open for 12% -> 13% of each run, Pallas kernels for 0% -> 0%
where the time goes in v1:
time: 450 us; the launch traced here: 443 us
  blocking collectives  142 us (32%)
  waiting for transfers between devices  137 us (30%)
  matrix products  89.5 us (20%)
  local copies, waits for them, and re-layouts  34.9 us (8%)
  starting transfers between devices  15.5 us (3%)
  between operations  14.6 us (3%)
  other arithmetic  9.61 us (2%)
    psum x1, blocking collectives, exchange_body(): joined = lax.psum(joined, ('seq', 'item'))[lax.axis_index('seq')]  74.8 us
    all_to_all x2, waiting for transfers between devices, mix(): packed = lax.all_to_all(packed, 'seq', 0, 2, tiled=True)  67.5 us
    reduce_scatter x1, waiting for transfers between devices, reduce_matrix(): cut = lax.psum_scatter(cut, 'seq', scatter_dimension=0, tiled=True)  56.7 us
    all_to_all x1, blocking collectives, mix(): lax.all_to_all(turned.astype(jnp.bfloat16), 'seq', 2, 0, tiled=True)  52.4 us
    dot_general x8, matrix products, plain_dot(): return jnp.dot(left, right, preferred_element_type=jnp.float32)  40 us
    dot_general x2, matrix products, cols_dot(): lax.dot_general(left, right, (((1,), (1,)), ((), ())), preferred_element_...  26 us
    all_gather x2, blocking collectives, reduce_matrix(): return lax.all_gather(cut, 'item', axis=1, tiled=True).astype(jnp.float32)  15.2 us
    unnamed x57, local copies, waits for them, and re-layouts  14.8 us
  transfers between devices with their start and end apart: 7, of which 6 were waited for; matrix products, arithmetic and copies ran while one was open for 13% of the time, Pallas kernels for 0%

profile of v1, /device:TPU:0, one launch (start us, length us, event | category | flops | bytes accessed | tf_op | source)
XLA Modules:
  0.0 443.3 jit_solution(398338748687127552)
XLA Ops:
  7.2 3.1 fusion.44
  10.3 2.0 copy.65
  12.3 7.3 %all-to-all-start = ((bf16[768,6,128]{2,1,0:T(8,128)(2,1)}), bf16[768,6,128]{2,1,0:T(8,128)(2,1)S(1)}, u32[]{:S(2)}, u32[]{:S(2)}) async-start(bf16[768,6,128]{2,1,0:T(8,128)(2,1)} %copy.65), calls=%async_computation | async-start | bytes 3145728 | tf_op jit(solution)/shard_map/all_to_all | solution.py:186
  19.6 36.9 %all-to-all-done = bf16[768,6,128]{2,1,0:T(8,128)(2,1)S(1)} async-done(((bf16[768,6,128]{2,1,0:T(8,128)(2,1)}), bf16[768,6,128]{2,1,0:T(8,128)(2,1)S(1)}, u32[]{:S(2)}, u32[]{:S(2)}) %all-to-all-start) | async-done | bytes 1179680 | tf_op jit(solution)/shard_map/all_to_all | solution.py:186
  56.6 1.4 copy.117
  58.1 0.3 slice.84
  58.4 2.4 fusion.48
  61.0 1.4 copy-done.4
  62.4 0.4 fusion.25
  62.9 0.3 slice.81
  63.2 2.4 fusion.47
  65.5 0.3 fusion.6
  65.9 2.1 copy.71
  68.0 52.4 %all_to_all.66 = bf16[96,6,1024]{0,1,2:T(8,128)(2,1)} all-to-all(bf16[96,6,1024]{0,1,2:T(8,128)(2,1)S(1)} %copy.71), channel_id=1, replica_groups=mesh['seq'=8,'item'=4] {'seq'}, dimensions={2} | all-to-all | bytes 2359296 | tf_op jit(solution)/shard_map/all_to_all | solution.py:192
  120.4 3.1 copy.73
  123.5 0.6 copy.74
  124.2 3.3 fusion.42
  127.6 0.4 multiply_reduce_fusion.4
  128.0 0.2 copy-done.12
  128.3 28.8 %multiply_convert_fusion = (bf16[768,3072]{1,0:T(8,128)(2,1)S(1)}, f32[768,3072]{1,0:T(8,128)}, f32[768,3072]{1,0:T(8,128)}) fusion(f32[3072]{0:T(1024)S(1)} %copy-done.15, f32[768,3072]{1,0:T(8,128)} %param.17, f32[768,768]{1,0:T(8,128)S(1)} %get-tuple-element.76, f32[768]{0:T(1024)S(1)} %copy-done.17, f32[768]{0:T(1024)S(1)} %copy-done.12, ...), kind=kOutput, calls=%fused_computation.4 | convolution fusion | flops 3784900608 | bytes 35414016 | tf_op jit(solution)/shard_map/dot_general | solution.py:17
  157.1 4.1 fusion.43
  161.3 0.4 multiply_reduce_fusion.3
  161.7 1.2 copy-done
  162.9 1.5 fusion.8
  164.4 2.4 fusion.39
  166.8 1.4 copy-done.3
  168.2 0.3 convert_reduce_fusion.1
  168.5 5.8 %convolution_convert_fusion = bf16[3072,768]{0,1:T(8,128)(2,1)} fusion(bf16[768,3072]{1,0:T(8,128)(2,1)S(1)} %get-tuple-element.63, bf16[768,768]{1,0:T(8,128)(2,1)S(1)} %get-tuple-element.56), kind=kOutput, calls=%fused_computation.18 | convolution fusion | flops 3626237952 | bytes 10616832 | tf_op jit(solution)/shard_map/dot_general | solution.py:21
  174.5 15.8 %convert_reduce_fusion = (f32[3072]{0:T(1024)}, bf16[768,3072]{1,0:T(8,128)(2,1)S(1)}) fusion(f32[768,3072]{1,0:T(8,128)} %get-tuple-element.64, bf16[768,768]{1,0:T(8,128)(2,1)S(1)} %get-tuple-element.56, f32[3072,768]{1,0:T(8,128)} %param.19, f32[768,3072]{1,0:T(8,128)} %get-tuple-element.77, f32[3072]{0:T(1024)} %param.18), kind=kOutput, calls=%fused_computation.2 | convolution fusion | flops 3666342912 | bytes 34234368 | tf_op jit(solution)/shard_map/dot_general | solution.py:27
  190.2 2.2 copy-done.22
  192.4 6.3 %convolution_convert_fusion.1 = bf16[768,3072]{1,0:T(8,128)(2,1)} fusion(bf16[768,3072]{1,0:T(8,128)(2,1)S(1)} %get-tuple-element.82, f32[768,768]{1,0:T(8,128)S(1)} %get-tuple-element.76, f32[768]{0:T(1024)S(1)} %copy-done.18, f32[768]{0:T(1024)S(1)} %copy-done.13, f32[768]{0:T(1024)S(1)} %fusion.32, f32[768]{0:T(1024)S(1)} %broadcast_multiply_fusion.1), kind=kOutput, calls=%fused_computation.19 | convolution fusion | flops 3629187072 | bytes 11808768 | tf_op jit(solution)/shard_map/dot_general | solution.py:21
  198.7 0.6 copy-done.7
  199.4 10.2 %multiply_reduce_fusion = (f32[768]{0:T(1024)S(1)}, f32[768]{0:T(1024)S(1)}, f32[768]{0:T(1024)S(1)}, f32[768,768]{1,0:T(8,128)S(1)}) fusion(f32[768,768]{1,0:T(8,128)S(1)} %get-tuple-element.76, f32[768]{0:T(1024)S(1)} %fusion.32, f32[768]{0:T(1024)S(1)} %broadcast_multiply_fusion.1, f32[768]{0:T(1024)S(1)} %copy-done.14, ...), kind=kOutput, calls=%fused_computation.31 | convolution fusion | flops 3632133888 | bytes 21255168 | tf_op jit(solution)/shard_map/dot_general | solution.py:27
  209.6 0.9 fusion.38
  210.5 1.7 fusion.37
  212.3 1.1 fusion.24
  213.4 2.0 copy.75
  215.3 3.6 all-to-all-start.2
  219.0 2.4 reduce-scatter.11.cloned.1.call-done
  221.4 2.8 copy.90
  224.2 30.5 %all-to-all-done.2 = bf16[768,6,128]{2,1,0:T(8,128)(2,1)S(1)} async-done(((bf16[768,6,128]{2,1,0:T(8,128)(2,1)}), bf16[768,6,128]{2,1,0:T(8,128)(2,1)S(1)}, u32[]{:S(2)}, u32[]{:S(2)}) %all-to-all-start.2) | async-done | bytes 1179680 | tf_op jit(solution)/shard_map/all_to_all | solution.py:186
  255.0 1.3 copy-done.20
  256.3 0.8 fusion.26
  257.4 0.5 copy-done.5
  257.9 0.4 convolution_select_fusion
  258.3 0.6 copy-done.19
  258.9 0.8 fusion.29
  259.7 0.3 fusion.7
  260.0 2.9 copy.80
  262.9 4.5 %all-to-all-start.3 = ((bf16[96,6,1024]{0,1,2:T(8,128)(2,1)}), bf16[96,6,1024]{0,1,2:T(8,128)(2,1)}, u32[]{:S(2)}, u32[]{:S(2)}) async-start(bf16[96,6,1024]{0,1,2:T(8,128)(2,1)} %copy.80), calls=%async_computation.3 | async-start | bytes 4194304 | tf_op jit(solution)/shard_map/all_to_all | solution.py:192
  267.5 4.6 %reduce-scatter.7.cloned.1.call-done = bf16[768,768]{1,0:T(8,128)(2,1)} async-done(((bf16[768,3072]{1,0:T(8,128)(2,1)}), bf16[768,768]{1,0:T(8,128)(2,1)}) %reduce-scatter.7.cloned.1.call-update) | async-done | bytes 1179664 | tf_op jit(solution)/shard_map/reduce_scatter | solution.py:230
  272.1 0.2 reduce_sum.146
  272.7 74.8 %psum.7 = f32[8,864]{1,0:T(8,128)S(1)} all-reduce(f32[8,864]{1,0:T(8,128)S(1)} %concatenate.11), channel_id=1, replica_groups=mesh['seq'=8,'item'=4] {'seq','item'}, use_global_device_ids=true, to_apply=%region_16.17 | all-reduce | flops 6912 | bytes 55296 | tf_op jit(solution)/shard_map/psum | solution.py:237
  347.5 0.6 dynamic-slice_reduce_fusion
  348.1 0.6 dynamic-slice_bitcast_fusion
  348.7 3.1 copy.82
  351.8 3.8 add_bitcast_fusion
  355.6 5.5 %reduce-scatter.13.cloned.1.call-done = bf16[384,192]{1,0:T(8,128)(2,1)} async-done(((bf16[3072,192]{1,0:T(8,128)(2,1)}), bf16[384,192]{1,0:T(8,128)(2,1)}) %reduce-scatter.13.cloned.1.call-update) | async-done | bytes 147472
  361.2 1.1 copy.91
  362.2 7.5 %all_gather.7 = bf16[384,768]{0,1:T(8,128)(2,1)S(1)} all-gather(bf16[384,192]{0,1:T(8,128)(2,1)S(1)} %copy.91), channel_id=1, replica_groups=mesh['seq'=8,'item'=4] {'item'}, dimensions={1}, use_global_device_ids=true | all-gather | bytes 737280 | tf_op jit(solution)/shard_map/all_gather | solution.py:232
  369.7 1.3 copy.84
  371.0 56.7 %reduce-scatter.9.cloned.1.call-done = bf16[96,768]{1,0:T(8,128)(2,1)} async-done(((bf16[768,768]{1,0:T(8,128)(2,1)}), bf16[96,768]{1,0:T(8,128)(2,1)}) %reduce-scatter.9.cloned.1.call-update) | async-done | bytes 147472 | tf_op jit(solution)/shard_map/reduce_scatter | solution.py:231
  427.7 7.7 %all_gather.6 = bf16[96,3072]{1,0:T(8,128)(2,1)S(1)} all-gather(bf16[96,768]{1,0:T(8,128)(2,1)} %reduce-scatter.9.cloned.1.call-done), channel_id=1, replica_groups=mesh['seq'=8,'item'=4] {'item'}, dimensions={1}, use_global_device_ids=true | all-gather | bytes 737280 | tf_op jit(solution)/shard_map/all_gather | solution.py:232
  435.4 1.1 convert_element_type.71
  (81 shorter events, 1.8 us)
Async XLA Ops:
  12.3 44.3 %all-to-all-start = ((bf16[768,6,128]{2,1,0:T(8,128)(2,1)}), bf16[768,6,128]{2,1,0:T(8,128)(2,1)S(1)}, u32[]{:S(2)}, u32[]{:S(2)}) async-start(bf16[768,6,128]{2,1,0:T(8,128)(2,1)} %copy.65), calls=%async_computation | async-start | bytes 3145728 | tf_op jit(solution)/shard_map/all_to_all | solution.py:186
  19.6 201.9 %reduce-scatter.11.cloned.1.call-start = ((), (), s32[]{:S(2)}) async-start(), calls=%async_computation.10 | async-start | bytes 5898240 | tf_op jit(solution)/shard_map/reduce_scatter | solution.py:230
  60.8 1.6 copy-start.4
  124.1 32.9 %slice-start = ((s8[9437184]{0:T(1024)(128)(4,1)}), s8[4194304]{0:T(1024)(128)(4,1)S(1)}, s32[]{:S(2)}) async-start(s8[9437184]{0:T(1024)(128)(4,1)} %bitcast.143), calls=%async_computation.12 | async-start | bytes 8388608
  127.5 0.7 copy-start.12
  127.5 0.7 copy-start.15
  127.5 0.7 copy-start.17
  128.2 28.8 %slice-start.1 = ((s8[9437184]{0:T(1024)(128)(4,1)}), s8[4194304]{0:T(1024)(128)(4,1)S(1)}, s32[]{:S(2)}) async-start(s8[9437184]{0:T(1024)(128)(4,1)} %bitcast.143), calls=%async_computation.13 | async-start | bytes 8388608
  128.2 28.9 %slice-start.2 = ((s8[9437184]{0:T(1024)(128)(4,1)}), s8[1048576]{0:T(1024)(128)(4,1)S(1)}, s32[]{:S(2)}) async-start(s8[9437184]{0:T(1024)(128)(4,1)} %bitcast.143), calls=%async_computation.14 | async-start | bytes 2097152
  128.2 28.9 %copy-start.16 = (f32[768]{0:T(1024)S(1)}, f32[768]{0:T(1024)}, u32[]{:S(2)}) copy-start(f32[768]{0:T(1024)} %param.20) | copy-start | bytes 9220
  161.2 1.7 copy-start
  161.2 1.7 copy-start.8
  162.9 1.5 copy-start.11
  166.8 1.4 copy-start.3
  166.8 1.7 copy-start.6
  174.4 97.7 %reduce-scatter.7.cloned.1.call-start = ((), (), s32[]{:S(2)}) async-start(), calls=%async_computation.8 | async-start | bytes 5898240 | tf_op jit(solution)/shard_map/reduce_scatter | solution.py:230
  174.4 18.0 %copy-start.13 = (f32[768]{0:T(1024)S(1)}, f32[768]{0:T(1024)}, u32[]{:S(2)}) copy-start(f32[768]{0:T(1024)} %param.21) | copy-start | bytes 9220
  174.4 18.0 %copy-start.18 = (f32[768]{0:T(1024)S(1)}, f32[768]{0:T(1024)}, u32[]{:S(2)}) copy-start(f32[768]{0:T(1024)} %param.22) | copy-start | bytes 9220
  190.2 2.2 copy-start.22
  198.7 0.7 copy-start.7
  198.7 0.7 copy-start.14
  210.5 1.7 copy-start.21
  215.3 39.4 %all-to-all-start.2 = ((bf16[768,6,128]{2,1,0:T(8,128)(2,1)}), bf16[768,6,128]{2,1,0:T(8,128)(2,1)S(1)}, u32[]{:S(2)}, u32[]{:S(2)}) async-start(bf16[768,6,128]{2,1,0:T(8,128)(2,1)} %copy.75), calls=%async_computation.2 | async-start | bytes 3145728 | tf_op jit(solution)/shard_map/all_to_all | solution.py:186
  218.9 142.2 %reduce-scatter.13.cloned.1.call-start = ((), (), s32[]{:S(2)}) async-start(), calls=%async_computation.11 | async-start | bytes 1769472
  254.7 1.6 copy-start.20
  256.3 1.6 copy-start.5
  257.1 1.8 copy-start.19
  262.9 9.2 %copy-start.1 = (f32[128,6,768]{2,0,1:T(8,128)S(1)}, f32[128,6,768]{2,0,1:T(8,128)}, u32[]{:S(2)}) copy-start(f32[128,6,768]{2,0,1:T(8,128)} %param.25) | copy-start | bytes 7077892
  262.9 85.8 %all-to-all-start.3 = ((bf16[96,6,1024]{0,1,2:T(8,128)(2,1)}), bf16[96,6,1024]{0,1,2:T(8,128)(2,1)}, u32[]{:S(2)}, u32[]{:S(2)}) async-start(bf16[96,6,1024]{0,1,2:T(8,128)(2,1)} %copy.80), calls=%async_computation.3 | async-start | bytes 4194304 | tf_op jit(solution)/shard_map/all_to_all | solution.py:192
  267.4 5.1 %copy-start.10 = (f32[3072]{0:T(1024)S(1)}, f32[3072]{0:T(1024)}, u32[]{:S(2)}) copy-start(f32[3072]{0:T(1024)} %get-tuple-element.81) | copy-start | bytes 36868
  267.4 5.2 %copy-start.9 = (f32[768]{0:T(1024)S(1)}, f32[768]{0:T(1024)}, u32[]{:S(2)}) copy-start(f32[768]{0:T(1024)} %get-tuple-element.50) | copy-start | bytes 9220
  267.4 160.3 %reduce-scatter.9.cloned.1.call-start = ((), (), s32[]{:S(2)}) async-start(), calls=%async_computation.9 | async-start | bytes 1327104 | tf_op jit(solution)/shard_map/reduce_scatter | solution.py:231
  272.3 79.6 %copy-start.2 = (f32[768,768]{1,0:T(8,128)S(1)}, f32[768,768]{1,0:T(8,128)}, u32[]{:S(2)}) copy-start(f32[768,768]{1,0:T(8,128)} %get-tuple-element.58) | copy-start | bytes 7077892
Sparse Core Ops, SparseCore 0:
  174.5 46.8 reduce-scatter.10
  224.1 47.8 reduce-scatter.6
  275.5 85.6 reduce-scatter.12
  364.8 62.8 reduce-scatter.8

commit v2 on v0

--- a/solution.py
+++ b/solution.py
@@ -2,7 +2,10 @@
 
 import jax
 import jax.numpy as jnp
+import numpy as np
 from jax import lax
+from jax.experimental import pallas as pl
+from jax.experimental.pallas import tpu as pltpu
 from jax.sharding import PartitionSpec as P
 
 
@@ -39,7 +42,7 @@
     return jax.nn.gelu(values, approximate=False)
 
 
-def body(inputs, w_in, c_in, w_out, c_out, gain_mix, bias_mix, gain_out, bias_out, cotangent):
+def gather_body(inputs, w_in, c_in, w_out, c_out, gain_mix, bias_mix, gain_out, bias_out, cotangent):
     local_len, per_dev, features = inputs.shape
     merged = per_dev * features
     period = local_len * lax.axis_size("seq")
@@ -145,6 +148,567 @@
     )
 
 
+def packed_tables(features, parts):
+    half = features // 2
+    share = half // parts
+    index = np.arange(features)
+    forward = np.zeros((features, features), np.float32)
+    unpack = np.zeros((features, features), np.float32)
+    for low in range(half):
+        block, place = divmod(low, share)
+        cos_slot = block * 2 * share + place
+        sin_slot = cos_slot + share
+        angles = (index * low % features).astype(np.float32) * np.float32(2.0 * math.pi / features)
+        forward[cos_slot] = np.cos(angles)
+        unpack[cos_slot, low] = 1.0
+        if low:
+            unpack[cos_slot, features - low] = 1.0
+            forward[sin_slot] = np.sin(angles)
+            unpack[sin_slot, low] = -1.0
+            unpack[sin_slot, features - low] = 1.0
+        else:
+            forward[sin_slot] = 1.0 - 2.0 * (index % 2)
+            unpack[sin_slot, half] = 1.0
+    return forward.astype(jnp.bfloat16), unpack.astype(jnp.bfloat16)
+
+
+def seq_tables(period):
+    index = np.arange(period)
+    angles = (index[:, None] * index[None, :] % period).astype(np.float32)
+    angles = angles * np.float32(2.0 * math.pi / period)
+    return np.cos(angles).astype(jnp.bfloat16), np.sin(angles).astype(jnp.bfloat16)
+
+
+MESH = pl.DeviceIdType.MESH
+CHUNKS = 3
+BF16, F32 = jnp.bfloat16, jnp.float32
+
+
+def dot(left, right, left_dim, right_dim):
+    return lax.dot_general(
+        left, right, (((left_dim,), (right_dim,)), ((), ())), preferred_element_type=F32
+    )
+
+
+def row_mean(values):
+    return jnp.mean(values, axis=-1, keepdims=True)
+
+
+def layer_kernel(
+    x_hbm, cot_hbm, win_hbm, wout_hbm, prm_hbm, fwd_hbm, unp_hbm, cos_hbm, sin_hbm,
+    out_hbm, gin_hbm, gmat_hbm, gvec_ref,
+    fwd_v, unp_v, cos_v, sin_v, prm_v, xbuf, cotb, wbuf, stage,
+    ysend, yrecv, zsend, zrecv, actb, gpb, hb, gbb, dgb, acc, r1b, ostage, vacc,
+    recv1, recv2, recv3, recv4, recv5, recv6, vsend, vrecv, vmid, vlast,
+    ld_sem, x_sem, cot_sem, stg_sem, a_send, a_recv, b_send, b_recv, out_sem,
+    red_send, red_recv, gat_send, gat_recv, v_send, v_recv,
+):
+    chunks, rows, features = xbuf.shape
+    per_chunk, share, period = yrecv.shape[2], yrecv.shape[3], yrecv.shape[4]
+    own_len = period // 8
+    half = share // 2
+    unit_scale = 1.0 / math.sqrt(period * features)
+
+    me, item = lax.axis_index("seq"), lax.axis_index("item")
+    peers = [(lax.rem(me + k, 8), item) for k in range(1, 8)]
+    z_lo, y_at = lax.rem(lax.div(me, 2), 2), lax.rem(me, 2)
+    z_at, z_hi = lax.div(me, 2), lax.div(me, 4)
+    core, x_at = lax.rem(item, 2), lax.div(item, 2)
+    core_peer = (me, item + 1 - 2 * core)
+    x_peer = (me, item + 2 - 4 * x_at)
+    far_peer = (me, lax.rem(item + 2, 4) + 1 - 2 * core)
+    y_peer = (me + 1 - 2 * y_at, item)
+    za_peer = (me + 2 - 4 * z_lo, item)
+    zb_peer = (me + 4 - 8 * z_hi, item)
+
+    def remote(src, dst, send, recv, peer):
+        return pltpu.make_async_remote_copy(
+            src_ref=src, dst_ref=dst, send_sem=send, recv_sem=recv, device_id=peer, device_id_type=MESH
+        )
+
+    def wait_bytes(ref, sem):
+        pltpu.make_async_copy(ref, ref, sem).wait()
+
+    tables = [
+        pltpu.make_async_copy(src, dst, ld_sem.at[i])
+        for i, (src, dst) in enumerate(
+            [(fwd_hbm, fwd_v), (prm_hbm, prm_v), (cos_hbm, cos_v), (sin_hbm, sin_v), (unp_hbm, unp_v)]
+        )
+    ]
+    x_loads = [pltpu.make_async_copy(x_hbm.at[c], xbuf.at[c], x_sem.at[c]) for c in range(chunks)]
+    cot_loads = [pltpu.make_async_copy(cot_hbm.at[c], cotb.at[c], cot_sem.at[c]) for c in range(chunks)]
+    x_loads[0].start()
+    tables[0].start()
+    for load in x_loads[1:] + tables[1:]:
+        load.start()
+
+    barrier = pltpu.get_barrier_semaphore()
+    everyone = peers + [core_peer, x_peer, far_peer]
+    for peer in everyone:
+        pl.semaphore_signal(barrier, inc=1, device_id=peer, device_id_type=MESH)
+
+    slots, piece = stage.shape[0], stage.shape[1]
+    per_block = features // piece
+    steps = 8 * per_block
+
+    def weight_load(step, part, slot):
+        block, at = lax.div(step, per_block), lax.rem(step, per_block) * piece
+        if part == 0:
+            cols = pl.ds(pl.multiple_of(block * features, features), features)
+            src = win_hbm.at[pl.ds(pl.multiple_of(at, piece), piece), cols]
+        else:
+            src = wout_hbm.at[pl.ds(pl.multiple_of(block * features + at, piece), piece), :]
+        return pltpu.make_async_copy(src, stage.at[slot], stg_sem.at[slot])
+
+    def cast_weights(part):
+        total = 4 * per_block
+        groups = piece // share
+
+        def one(step, carry):
+            slot = lax.rem(step, slots)
+            weight_load(step, part, slot).wait()
+            block, at = lax.div(step, per_block), lax.rem(step, per_block) * groups
+            value = stage[slot].astype(BF16)
+            for g in range(groups):
+                where = at + g
+                wbuf[4 * part + block, lax.div(where, 2), lax.rem(where, 2)] = value[g * share : (g + 1) * share]
+
+            @pl.when(step + slots < total)
+            def _():
+                weight_load(step + slots, part, slot).start()
+
+            return carry
+
+        lax.fori_loop(0, total, one, 0)
+
+    def first_loads(part):
+        for slot in range(slots):
+            weight_load(jnp.int32(slot), part, jnp.int32(slot)).start()
+
+    def block_of(index):
+        return wbuf[index].reshape(features, features)
+
+    def to_owners(turn, c, low):
+        packed = dot(fwd_v[...], low, 1, 1).astype(BF16)
+        for s in range(per_chunk):
+            ysend[c, s] = packed[:, s * own_len : (s + 1) * own_len]
+        mine = pl.ds(pl.multiple_of(me * own_len, own_len), own_len)
+        for peer in peers:
+            to = pl.ds(pl.multiple_of(peer[0] * share, share), share)
+            remote(
+                ysend.at[c, :, to, :], yrecv.at[turn, c, :, :, mine], a_send.at[turn, c], a_recv.at[turn, c], peer
+            ).start()
+        own = pl.ds(pl.multiple_of(me * share, share), share)
+        pltpu.make_async_copy(ysend.at[c, :, own, :], yrecv.at[turn, c, :, :, mine], a_recv.at[turn, c]).start()
+
+    def owners_sent(turn, c):
+        wait_bytes(ysend.at[c, :, pl.ds(0, 7 * share), :], a_send.at[turn, c])
+
+    def turn_and_return(turn, c):
+        wait_bytes(yrecv.at[turn, c], a_recv.at[turn, c])
+        held = yrecv[turn, c]
+        cos_rows = held[:, :half].reshape(per_chunk * half, period)
+        sin_rows = held[:, half:].reshape(per_chunk * half, period)
+        mid_rows = held[:, half : half + 16].reshape(per_chunk * 16, period)
+        by_cos = dot(cos_rows, cos_v[...], 1, 0) * unit_scale
+        by_sin = dot(sin_rows, sin_v[...], 1, 0) * unit_scale
+        by_mid = dot(mid_rows, cos_v[...], 1, 0) * unit_scale
+        top = lax.broadcasted_iota(jnp.int32, (16, period), 0) == 0
+        top = jnp.logical_and(top, me == 0)
+        for s in range(per_chunk):
+            zsend[c, s, :half] = by_cos[s * half : (s + 1) * half].astype(BF16)
+            sin_part = by_sin[s * half : (s + 1) * half]
+            zsend[c, s, half : half + 16] = jnp.where(
+                top, by_mid[s * 16 : (s + 1) * 16], sin_part[:16]
+            ).astype(BF16)
+            zsend[c, s, half + 16 :] = sin_part[16:].astype(BF16)
+        mine = pl.ds(pl.multiple_of(me * share, share), share)
+        for peer in peers:
+            to = pl.ds(pl.multiple_of(peer[0] * own_len, own_len), own_len)
+            remote(
+                zsend.at[c, :, :, to], zrecv.at[turn, c, :, mine, :], b_send.at[turn, c], b_recv.at[turn, c], peer
+            ).start()
+        own = pl.ds(pl.multiple_of(me * own_len, own_len), own_len)
+        pltpu.make_async_copy(zsend.at[c, :, :, own], zrecv.at[turn, c, :, mine, :], b_recv.at[turn, c]).start()
+
+    def return_sent(turn, c):
+        wait_bytes(zsend.at[c, :, :, pl.ds(0, 7 * own_len)], b_send.at[turn, c])
+
+    def mixed_of(turn, c):
+        wait_bytes(zrecv.at[turn, c], b_recv.at[turn, c])
+        held = jnp.concatenate([zrecv[turn, c, s] for s in range(per_chunk)], axis=1)
+        return dot(held, unp_v[...], 0, 0)
+
+    tables[0].wait()
+    for c in range(chunks):
+        x_loads[c].wait()
+        if c == 0:
+            first_loads(0)
+            pl.semaphore_wait(barrier, len(everyone))
+        to_owners(0, c, xbuf[c].astype(BF16))
+    for load in tables[1:]:
+        load.wait()
+    for load in cot_loads:
+        load.start()
+    vacc[...] = jnp.zeros_like(vacc)
+    cast_weights(0)
+    first_loads(1)
+    for c in range(chunks):
+        turn_and_return(0, c)
+        if c == 0:
+            cast_weights(1)
+    for load in cot_loads:
+        load.wait()
+    for c in range(chunks):
+        owners_sent(0, c)
+
+    gain_mix, bias_mix = prm_v[5:6], prm_v[6:7]
+    gain_out, bias_out, c_out = prm_v[7:8], prm_v[8:9], prm_v[4:5]
+
+    def out_copy(c):
+        return pltpu.make_async_copy(ostage, out_hbm.at[c], out_sem.at[0])
+
+    def feed(c, carry):
+        value = xbuf[c] + mixed_of(0, c)
+        value = value - row_mean(value)
+        scale = lax.rsqrt(row_mean(value * value) + 1e-05)
+        normal = value * scale
+        r1b[...] = jnp.broadcast_to(scale, r1b.shape)
+        xbuf[c] = normal
+        hidden = normal * gain_mix + bias_mix
+        hb[c] = hidden.astype(BF16)
+        acc[...] = hidden + c_out
+
+        def up(j, carry):
+            pre = dot(hb[c], block_of(j), 1, 0) + prm_v[pl.ds(j, 1)]
+            prob = 0.5 + 0.5 * lax.erf(pre * math.sqrt(0.5))
+            density = jnp.exp(-0.5 * pre * pre) * (1.0 / math.sqrt(2.0 * math.pi))
+            act = (pre * prob).astype(BF16)
+            dgb[j] = prob + pre * density
+            actb[j, c] = act
+            acc[...] += dot(act, block_of(4 + j), 1, 0)
+            return carry
+
+        lax.fori_loop(0, 4, up, 0)
+        value = acc[...]
+        value = value - row_mean(value)
+        scale = lax.rsqrt(row_mean(value * value) + 1e-05)
+        normal = value * scale
+
+        @pl.when(c > 0)
+        def _():
+            out_copy(c).wait()
+
+        ostage[...] = normal * gain_out + bias_out
+        out_copy(c).start()
+        cot = cotb[c]
+        vacc[7:8] += jnp.sum(cot * normal, axis=0, keepdims=True)
+        vacc[8:9] += jnp.sum(cot, axis=0, keepdims=True)
+        scaled = cot * gain_out
+        g_sum2 = scale * (scaled - row_mean(scaled) - normal * row_mean(scaled * normal))
+        low = g_sum2.astype(BF16)
+        gbb[c] = low
+        vacc[4:5] += jnp.sum(low.astype(F32), axis=0, keepdims=True)
+        acc[...] = g_sum2
+
+        def down(j, carry):
+            g_pre = (dot(gbb[c], block_of(4 + j), 1, 1) * dgb[j]).astype(BF16)
+            gpb[j, c] = g_pre
+            vacc[pl.ds(j, 1)] += jnp.sum(g_pre.astype(F32), axis=0, keepdims=True)
+            acc[...] += dot(g_pre, block_of(j), 1, 1)
+            return carry
+
+        lax.fori_loop(0, 4, down, 0)
+        g_hidden = acc[...]
+        normal = xbuf[c]
+        vacc[5:6] += jnp.sum(g_hidden * normal, axis=0, keepdims=True)
+        vacc[6:7] += jnp.sum(g_hidden, axis=0, keepdims=True)
+        scaled = g_hidden * gain_mix
+        g_sum1 = r1b[:, :1] * (scaled - row_mean(scaled) - normal * row_mean(scaled * normal))
+        xbuf[c] = g_sum1
+        to_owners(1, c, g_sum1.astype(BF16))
+        return carry
+
+    lax.fori_loop(0, chunks, feed, 0)
+
+    lanes = vsend.shape[2]
+    vsend[...] = jnp.zeros_like(vsend)
+    for d in range(8):
+        at = d * (features // 2)
+        for r in range(3):
+            where = at + r * lanes
+            vsend[d, r : r + 1, :] = vacc[where // features : where // features + 1, where % features : where % features + lanes]
+        for r in range(5):
+            vsend[d, 3 + r : 4 + r, :share] = vacc[4 + r : 5 + r, d * share : (d + 1) * share]
+    for peer in peers:
+        remote(vsend.at[peer[0]], vrecv.at[me], v_send.at[0], v_recv.at[0], peer).start()
+    pltpu.make_async_copy(vsend.at[me], vrecv.at[me], v_recv.at[0]).start()
+
+    def weight_products(kind):
+        def one(j, carry):
+            if kind == 0:
+                grad = dot(hb[...].reshape(-1, features), gpb[j].reshape(-1, features), 0, 0)
+                wbuf[j] = grad.astype(BF16).reshape(wbuf.shape[1:])
+            else:
+                grad = dot(actb[j].reshape(-1, features), gbb[...].reshape(-1, features), 0, 0).astype(BF16)
+                for y in range(2):
+                    for q in range(4):
+                        at = (y * 4 + q) * share
+                        wbuf[4 + q, j, y] = grad[at : at + share]
+            return carry
+
+        lax.fori_loop(0, 4, one, 0)
+
+    def core_send(kind):
+        for x in range(2):
+            remote(
+                wbuf.at[4 * kind + 2 * x + 1 - core], recv1.at[kind, x],
+                red_send.at[0, kind], red_recv.at[0, kind], core_peer,
+            ).start()
+
+    def core_sum(kind):
+        wait_bytes(recv1.at[kind], red_recv.at[0, kind])
+        for x in range(2):
+            wbuf[4 * kind + 2 * x + core] += recv1[kind, x]
+
+    def second_send(kind):
+        if kind == 0:
+            remote(
+                wbuf.at[2 * (1 - x_at) + core], recv2.at[0], red_send.at[1, 0], red_recv.at[1, 0], x_peer
+            ).start()
+        else:
+            for x in range(2):
+                remote(
+                    wbuf.at[4 + 2 * x + core, :, 1 - y_at], recv2.at[1, :, x],
+                    red_send.at[1, 1], red_recv.at[1, 1], y_peer,
+                ).start()
+
+    def second_sum(kind):
+        wait_bytes(recv2.at[kind], red_recv.at[1, kind])
+        if kind == 0:
+            wbuf[2 * x_at + core] += recv2[0]
+        else:
+            for x in range(2):
+                wbuf[4 + 2 * x + core, :, y_at] += recv2[1, :, x]
+
+    own_block = [2 * x_at + core, 4 + 2 * x_at + core]
+
+    def third_send(kind):
+        if kind == 0:
+            src, peer = wbuf.at[own_block[0], :, 1 - y_at], y_peer
+        else:
+            src, peer = wbuf.at[4 + 2 * (1 - x_at) + core, :, y_at], x_peer
+        remote(src, recv3.at[kind], red_send.at[2, kind], red_recv.at[2, kind], peer).start()
+
+    def third_sum(kind):
+        wait_bytes(recv3.at[kind], red_recv.at[2, kind])
+        wbuf[own_block[kind], :, y_at] += recv3[kind]
+
+    z_pair = lax.rem(z_at + 2, 4)
+    z_next = z_at + 1 - 2 * z_lo
+
+    def fourth_send(kind):
+        for slot, z in ((0, z_next), (1, lax.rem(z_next + 2, 4))):
+            remote(
+                wbuf.at[own_block[kind], z, y_at], recv4.at[kind, slot],
+                red_send.at[3, kind], red_recv.at[3, kind], za_peer,
+            ).start()
+
+    def fourth_sum(kind):
+        wait_bytes(recv4.at[kind], red_recv.at[3, kind])
+        for slot, z in ((0, z_at), (1, z_pair)):
+            wbuf[own_block[kind], z, y_at] += recv4[kind, slot]
+
+    def fifth_send(kind):
+        remote(
+            wbuf.at[own_block[kind], z_pair, y_at], recv5.at[kind], red_send.at[4, kind], red_recv.at[4, kind], zb_peer
+        ).start()
+
+    def fifth_sum(kind):
+        wait_bytes(recv5.at[kind], red_recv.at[4, kind])
+        recv6[kind, item] = wbuf[own_block[kind], z_at, y_at] + recv5[kind]
+        for peer in (x_peer, core_peer, far_peer):
+            remote(
+                recv6.at[kind, item], recv6.at[kind, item], gat_send.at[kind], gat_recv.at[kind], peer
+            ).start()
+
+    def mat_copy(kind):
+        return pltpu.make_async_copy(recv6.at[kind], gmat_hbm.at[kind], out_sem.at[2])
+
+    def gathered(kind):
+        wait_bytes(recv6.at[kind, pl.ds(0, 3)], gat_recv.at[kind])
+
+    def final(c):
+        grad = xbuf[c] + mixed_of(1, c)
+        xbuf[c] = grad
+        pltpu.make_async_copy(xbuf.at[c], gin_hbm.at[c], out_sem.at[1]).start()
+
+    weight_products(0)
+    core_send(0)
+    for c in range(chunks):
+        return_sent(0, c)
+    turn_and_return(1, 0)
+    weight_products(1)
+    core_send(1)
+    core_sum(0)
+    second_send(0)
+    turn_and_return(1, 1)
+    core_sum(1)
+    second_send(1)
+    turn_and_return(1, 2)
+
+    wait_bytes(vrecv, v_recv.at[0])
+    vmid[...] = jnp.sum(vrecv[...], axis=0)
+    for peer in (x_peer, core_peer, far_peer):
+        remote(vmid, vlast.at[item], v_send.at[1], v_recv.at[1], peer).start()
+    pltpu.make_async_copy(vmid, vlast.at[item], v_recv.at[1]).start()
+
+    second_sum(0)
+    third_send(0)
+    second_sum(1)
+    third_send(1)
+    final(0)
+    third_sum(0)
+    fourth_send(0)
+    third_sum(1)
+    fourth_send(1)
+    final(1)
+    fourth_sum(0)
+    fifth_send(0)
+    fourth_sum(1)
+    fifth_send(1)
+    fifth_sum(0)
+    fifth_sum(1)
+    wait_bytes(vlast, v_recv.at[1])
+    gvec_ref[...] = jnp.sum(vlast[...], axis=0)
+    final(2)
+    for kind in range(2):
+        gathered(kind)
+        mat_copy(kind).start()
+
+    out_copy(chunks - 1).wait()
+    wait_bytes(xbuf, out_sem.at[1])
+    wait_bytes(recv6, out_sem.at[2])
+    for c in range(chunks):
+        owners_sent(1, c)
+        return_sent(1, c)
+    for kind in range(2):
+        wait_bytes(recv1.at[kind], red_send.at[0, kind])
+        wait_bytes(recv2.at[kind], red_send.at[1, kind])
+        wait_bytes(recv3.at[kind], red_send.at[2, kind])
+        wait_bytes(recv4.at[kind], red_send.at[3, kind])
+        wait_bytes(recv5.at[kind], red_send.at[4, kind])
+        wait_bytes(recv6.at[kind, pl.ds(0, 3)], gat_send.at[kind])
+    wait_bytes(vrecv.at[pl.ds(0, 7)], v_send.at[0])
+    wait_bytes(vlast.at[pl.ds(0, 3)], v_send.at[1])
+
+
+def exchange_body(inputs, w_in, c_in, w_out, c_out, gain_mix, bias_mix, gain_out, bias_out, cotangent):
+    local_len, per_dev, features = inputs.shape
+    parts = lax.axis_size("seq")
+    period = local_len * parts
+    share = features // parts
+    per_chunk = per_dev // CHUNKS
+    rows = per_chunk * local_len
+    forward, unpack = packed_tables(features, parts)
+    cos_seq, sin_seq = seq_tables(period)
+    held = jnp.swapaxes(inputs, 0, 1).reshape(CHUNKS, rows, features)
+    cot = jnp.swapaxes(cotangent, 0, 1).reshape(CHUNKS, rows, features)
+    params = jnp.concatenate(
+        [c_in.reshape(4, features)]
+        + [v[None] for v in (c_out, gain_mix, bias_mix, gain_out, bias_out)]
+        + [jnp.zeros((7, features), F32)],
+        axis=0,
+    )
+    anywhere = pl.BlockSpec(memory_space=pl.ANY)
+    whole = (CHUNKS, rows, features)
+    vm, dma = pltpu.VMEM, pltpu.SemaphoreType.DMA
+    output, grad_inputs, mats, vecs = pl.pallas_call(
+        layer_kernel,
+        out_shape=(
+            jax.ShapeDtypeStruct(whole, F32),
+            jax.ShapeDtypeStruct(whole, F32),
+            jax.ShapeDtypeStruct((2, 4, share, features), BF16),
+            jax.ShapeDtypeStruct((8, 128), F32),
+        ),
+        in_specs=[anywhere] * 9,
+        out_specs=(anywhere, anywhere, anywhere, pl.BlockSpec(memory_space=pltpu.VMEM)),
+        scratch_shapes=[
+            vm((features, features), BF16),
+            vm((features, features), BF16),
+            vm((period, period), BF16),
+            vm((period, period), BF16),
+            vm((16, features), F32),
+            vm(whole, F32),
+            vm(whole, F32),
+            vm((8, 4, 2, share, features), BF16),
+            vm((4, 192, features), F32),
+            vm((CHUNKS, per_chunk, features, local_len), BF16),
+            vm((2, CHUNKS, per_chunk, share, period), BF16),
+            vm((CHUNKS, per_chunk, share, period), BF16),
+            vm((2, CHUNKS, per_chunk, features, local_len), BF16),
+            vm((4,) + whole, BF16),
+            vm((4,) + whole, BF16),
+            vm(whole, BF16),
+            vm(whole, BF16),
+            vm((4, rows, features), F32),
+            vm((rows, features), F32),
+            vm((rows, 128), F32),
+            vm((rows, features), F32),
+            vm((16, features), F32),
+            vm((2, 2, 4, 2, share, features), BF16),
+            vm((2, 4, 2, share, features), BF16),
+            vm((2, 4, share, features), BF16),
+            vm((2, 2, share, features), BF16),
+            vm((2, share, features), BF16),
+            vm((2, 4, share, features), BF16),
+            vm((8, 8, 128), F32),
+            vm((8, 8, 128), F32),
+            vm((8, 128), F32),
+            vm((4, 8, 128), F32),
+            dma((5,)),
+            dma((CHUNKS,)),
+            dma((CHUNKS,)),
+            dma((4,)),
+            dma((2, CHUNKS)),
+            dma((2, CHUNKS)),
+            dma((2, CHUNKS)),
+            dma((2, CHUNKS)),
+            dma((3,)),
+            dma((5, 2)),
+            dma((5, 2)),
+            dma((2,)),
+            dma((2,)),
+            dma((2,)),
+            dma((2,)),
+        ],
+        compiler_params=pltpu.CompilerParams(
+            collective_id=0, has_side_effects=True, vmem_limit_bytes=62 * 1024 * 1024
+        ),
+    )(held, cot, w_in, w_out, params, forward, unpack, cos_seq, sin_seq)
+    shape = (per_dev, local_len, features)
+    grad_in = jnp.swapaxes(mats[0], 0, 1).reshape(share, 4 * features).astype(F32)
+    grad_out = mats[1].reshape(4 * share, features).astype(F32)
+    return (
+        jnp.swapaxes(output.reshape(shape), 0, 1),
+        jnp.swapaxes(grad_inputs.reshape(shape), 0, 1),
+        grad_in,
+        vecs[:3].reshape(-1),
+        grad_out,
+        vecs[3, :share],
+        vecs[4, :share],
+        vecs[5, :share],
+        vecs[6, :share],
+        vecs[7, :share],
+    )
+
+
+def body(inputs, *rest):
+    if lax.axis_size("seq") != 8 or lax.axis_size("item") != 4:
+        return gather_body(inputs, *rest)
+    return exchange_body(inputs, *rest)
+
+
 def solution(mesh):
     placed = (
         P("seq", "item", None),

time: 833 us -> 192 us (0.23)
  waiting for transfers between devices: 508 us -> 0 us
  Pallas kernels: 0 us -> 176 us
  matrix products: 151 us -> 0 us
  local copies, waits for them, and re-layouts: 87.7 us -> 11.6 us
  blocking collectives: 41.6 us -> 0 us
  other arithmetic: 20.5 us -> 2.49 us
  between operations: 16.3 us -> 0.68 us
    all_gather x3 -> x0, waiting for transfers between devices: 350 us -> none  [the longest x1 119 us: body(): lax.all_gather(cos_part, 'seq', axis=0, tiled=True)]
    pallas_call x0 -> x1, Pallas kernels: none -> 176 us  [exchange_body(): pl.pallas_call(layer_kernel, out_shape=(jax.ShapeDtypeStruct(whole, F32),...]
    reduce_scatter x2 -> x0, waiting for transfers between devices: 157 us -> none  [the longest x1 98.5 us: body(): lax.psum_scatter(grad_w_in.astype(jnp.bfloat16), 'seq', scatter_dimension...]
    dot_general x14 -> x0, matrix products: 151 us -> none  [the longest x6 73.5 us: plain_dot(): return jnp.dot(left, right, preferred_element_type=jnp.float32)]
    all_gather x3 -> x0, local copies, waits for them, and re-layouts: 37.9 us -> none  [the longest x1 12.8 us: body(): lax.all_gather(cos_part, 'seq', axis=0, tiled=True)]
    unnamed x1 -> x0, blocking collectives: 35.9 us -> none
    reshape x13 -> x2, local copies, waits for them, and re-layouts: 26.7 us -> 1.3 us  [the longest x1 0.72 us: exchange_body(): c_in.reshape(4, features)]
    unnamed x64 -> x8, local copies, waits for them, and re-layouts: 20.7 us -> 3.93 us
  transfers between devices with their start and end apart: 6 -> 0, of which waited for: 5 -> 0; matrix products, arithmetic and copies ran while one was open for 12% -> 0% of each run, Pallas kernels for 0% -> 0%
where the time goes in v2:
time: 192 us; the launch traced here: 191 us
  Pallas kernels  176 us (92%)
  local copies, waits for them, and re-layouts  11.6 us (6%)
  other arithmetic  2.49 us (1%)
    pallas_call x1, Pallas kernels, exchange_body(): pl.pallas_call(layer_kernel, out_shape=(jax.ShapeDtypeStruct(whole, F32),...  176 us
    unnamed x8, local copies, waits for them, and re-layouts  3.93 us

profile of v2, /device:TPU:0, one launch (start us, length us, event | category | flops | bytes accessed | tf_op | source)
XLA Modules:
  0.0 190.8 jit_solution(13391887092688565597)
XLA Ops:
  0.6 0.7 reshape.47
  1.4 0.7 broadcast_in_dim.18
  2.1 0.7 broadcast_in_dim.19
  2.7 0.7 broadcast_in_dim.20
  3.4 0.7 broadcast_in_dim.21
  4.1 0.7 broadcast_in_dim.22
  4.8 1.3 concatenate.3.prm_hbm
  6.1 176.1 %shard_map.213 = (f32[3,256,768]{2,1,0:T(8,128)}, f32[3,256,768]{2,1,0:T(8,128)}, bf16[2,4,96,768]{3,2,1,0:T(8,128)(2,1)}, f32[8,128]{1,0:T(8,128)}) custom-call(f32[3,256,768]{2,1,0:T(8,128)} %bitcast.36, f32[3,256,768]{2,1,0:T(8,128)} %bitcast.37, f32[768,3072]{1,0:T(8,128)} %win_hbm.1, f32[3072,768]{1,0:T(8,128)} %wout_hbm.1, ...), custom_call_target="tpu_custom_call" | custom-call | tf_op jit(solution)/shard_map/pallas_call | solution.py:626
  182.1 0.0 copy-start.2
  182.1 1.4 fusion
  183.5 0.0 copy-start.1
  183.5 1.1 copy.25
  184.7 0.0 copy-done.2
  184.7 0.6 slice_bitcast_fusion
  185.2 1.1 bitcast_convert_fusion
  186.4 0.5 slice_bitcast_fusion.1
  186.9 0.0 copy-done.1
  186.9 0.0 copy-start
  186.9 1.4 copy.28
  188.3 1.1 copy-done
  189.4 1.4 copy.29
  (1 shorter events, 0.0 us)
Async XLA Ops:
  182.1 2.5 %copy-start.2 = (f32[8,128]{1,0:T(8,128)S(1)}, f32[8,128]{1,0:T(8,128)}, u32[]{:S(2)}) copy-start(f32[8,128]{1,0:T(8,128)} %get-tuple-element.17) | copy-start | bytes 12292
  183.5 3.4 %copy-start.1 = (f32[3,256,768]{2,1,0:T(8,128)S(1)}, f32[3,256,768]{2,1,0:T(8,128)}, u32[]{:S(2)}) copy-start(f32[3,256,768]{2,1,0:T(8,128)} %get-tuple-element.14) | copy-start | bytes 7077892
  186.9 2.5 %copy-start = (f32[3,256,768]{2,1,0:T(8,128)S(1)}, f32[3,256,768]{2,1,0:T(8,128)}, u32[]{:S(2)}) copy-start(f32[3,256,768]{2,1,0:T(8,128)} %get-tuple-element.15) | copy-start | bytes 7077892
